TPU v7x, 32 devices: a whole 2x2x4 slice. The times are simulated.
32 devices in a mesh: seq: 8 (over z, x), grp: 4 (over y, core).
Axes of the slice: x: 2, y: 2, z: 4, core: 2. Of those that a mesh axis runs over, the one named last changes fastest.
Arguments:
- tokens: bfloat16 [4096, 4096], P(('seq', 'grp')), may hold values from -8 to 8
- head_index: int32 [4096, 4], P(('seq', 'grp')), may hold values from 0 to 31, as said below
- gate_fixed: int32 [4096, 4], P(('seq', 'grp')), may hold values from 1 to 32767
- kv_weight: bfloat16 [4096, 4, 256], replicated, may hold values from -0.265625 to 0.265625
- query_weight: bfloat16 [4096, 4096], P('seq', 'grp'), may hold values from -0.265625 to 0.265625
- out_weight: bfloat16 [4096, 4096], P('grp', 'seq'), may hold values from -0.5 to 0.5
Outputs:
- mixed: bfloat16 [4096, 4096], P(('seq', 'grp'))
Inputs may be any that keep to these rules, and one draw needn't show every extreme that they name: `head_index`: each row names 4 different head experts lying in exactly 2 of the 4 groups (head e in group e // 8), at least one in each of the two.
All inputs are finite; a program needn't handle non-finite values.
Results may differ from a plain program's by a relative error of at most 0.013.
Values may be sent and summed in bfloat16 or wider, within the bound.
A program may use at most 192 MiB of HBM per device.

v0:
```python
import jax
import jax.numpy as jnp
from jax import lax
from jax.sharding import PartitionSpec as P


def route_tables(head_index, gate_fixed, groups, capacity, group_heads):
    slots = head_index.shape[1] - 1
    cluster_membership = head_index // group_heads
    local_head = head_index % group_heads
    in_group = cluster_membership[:, None, :] == jnp.arange(groups, dtype=jnp.int32)[None, :, None]
    slot_order = jnp.cumsum(in_group.astype(jnp.int32), axis=2) - 1
    picked = (
        in_group[:, :, :, None] & (slot_order[:, :, :, None] == jnp.arange(slots, dtype=jnp.int32))
    ).astype(jnp.int32)
    slot_head = jnp.sum(picked * local_head[:, None, :, None], axis=2)
    slot_gate = jnp.sum(picked * gate_fixed[:, None, :, None], axis=2)
    member = jnp.any(in_group, axis=2).astype(jnp.int32)
    ranking = jnp.cumsum(member, axis=0) - 1
    retained = (member > 0) & (ranking < capacity)
    selected = (
        retained[:, :, None] & (ranking[:, :, None] == jnp.arange(capacity, dtype=jnp.int32))
    ).astype(jnp.int32)
    return (selected, slot_head, slot_gate)


def attend(state, queries, query_pos, keys_values):
    key_count = keys_values.shape[0]
    head_width = queries.shape[1]
    key_block = 1024
    latest = jnp.max(query_pos)
    score_scale = head_width ** (-0.5)

    def update(carry, first_key, piece):
        running, total, accum = carry
        scores = (
            lax.dot_general(
                queries,
                piece[:, :head_width],
                (((1,), (1,)), ((), ())),
                preferred_element_type=jnp.float32,
            )
            * score_scale
        )
        key_pos = first_key + jnp.arange(key_block, dtype=jnp.int32)
        visible = key_pos[None, :] <= query_pos[:, None]
        scores = jnp.where(visible, scores, -1e30)
        newest = jnp.maximum(running, jnp.max(scores, axis=1))
        weights = jnp.where(visible, jnp.exp(scores - newest[:, None]), 0.0)
        factor = jnp.exp(running - newest)
        total = total * factor + jnp.sum(weights, axis=1)
        accum = accum * factor[:, None] + jnp.dot(
            weights.astype(jnp.bfloat16), piece[:, head_width:], preferred_element_type=jnp.float32
        )
        return (newest, total, accum)

    def step(carry, block_index):
        first_key = block_index * key_block
        piece = lax.dynamic_slice_in_dim(keys_values, block_index * key_block, key_block, 0)
        carry = lax.cond(
            first_key <= latest,
            lambda inner: update(inner, first_key, piece),
            lambda inner: inner,
            carry,
        )
        return (carry, None)

    state, _ = lax.scan(step, state, jnp.arange(key_count // key_block, dtype=jnp.int32))
    return state


def on_device(tokens, head_index, gate_fixed, kv_weight, query_weight, out_weight):
    groups = lax.axis_size("grp")
    tok_rows = tokens.shape[0]
    capacity = 3 * tok_rows // groups
    model_width = tokens.shape[1]
    head_width = kv_weight.shape[2] // 2
    group_heads = query_weight.shape[1] // head_width
    slots = head_index.shape[1] - 1
    offset = (lax.axis_index("seq") * groups + lax.axis_index("grp")) * tok_rows
    positions = offset + jnp.arange(tok_rows, dtype=jnp.int32)
    kv_local = jnp.einsum(
        "td,dgc->tgc", tokens, kv_weight, preferred_element_type=jnp.float32
    ).astype(jnp.bfloat16)
    selected, slot_head, slot_gate = route_tables(
        head_index, gate_fixed, groups, capacity, group_heads
    )
    by_slot = jnp.transpose(selected, (1, 2, 0))
    by_slot_bf = by_slot.astype(jnp.bfloat16)
    send_tokens = jnp.einsum(
        "gct,td->gcd", by_slot_bf, tokens, preferred_element_type=jnp.float32
    ).astype(jnp.bfloat16)
    send_pos = jnp.sum(by_slot * positions[None, None, :], axis=2)
    send_head = jnp.sum(
        by_slot[:, :, :, None] * jnp.transpose(slot_head, (1, 0, 2))[:, None, :, :], axis=2
    )
    send_gate = jnp.sum(
        by_slot[:, :, :, None] * jnp.transpose(slot_gate, (1, 0, 2))[:, None, :, :], axis=2
    )
    send_meta = jnp.concatenate([send_head, send_gate, send_pos[:, :, None]], axis=2)
    recv_tokens, recv_meta = (
        lax.all_to_all(send_tokens, "grp", split_axis=0, concat_axis=0, tiled=True),
        lax.all_to_all(send_meta, "grp", split_axis=0, concat_axis=0, tiled=True),
    )
    slot_rows = groups * capacity
    place_entries = recv_tokens.reshape(slot_rows, model_width)
    recv_meta = recv_meta.reshape(slot_rows, 2 * slots + 1)
    heads = recv_meta[:, :slots]
    gates = recv_meta[:, slots : 2 * slots].astype(jnp.float32) / 32768.0
    slot_pos = recv_meta[:, 2 * slots]
    q_all = jnp.dot(
        place_entries,
        lax.all_gather(query_weight, "seq", axis=0, tiled=True),
        preferred_element_type=jnp.float32,
    )
    indicator_vector = (heads[:, :, None] == jnp.arange(group_heads, dtype=jnp.int32)).astype(
        jnp.float32
    )
    queries = jnp.einsum(
        "rjh,rhd->rjd",
        indicator_vector,
        q_all.reshape(slot_rows, group_heads, head_width),
        precision=lax.Precision.HIGHEST,
    )
    queries = queries.astype(jnp.bfloat16).reshape(slot_rows * slots, head_width)
    query_pos = jnp.repeat(slot_pos, slots)
    total_rows = slot_rows * slots
    kv_group = lax.all_to_all(kv_local, "grp", split_axis=1, concat_axis=0, tiled=True).reshape(
        groups * tok_rows, 2 * head_width
    )
    final_state = attend(
        (
            jnp.full((total_rows,), -1e30, jnp.float32),
            jnp.zeros((total_rows,), jnp.float32),
            jnp.zeros((total_rows, head_width), jnp.float32),
        ),
        queries,
        query_pos,
        lax.all_gather(kv_group, "seq", axis=0, tiled=True),
    )
    head_out = final_state[2] / final_state[1][:, None]
    gated = head_out.reshape(slot_rows, slots, head_width) * gates[:, :, None]
    weighted = jnp.einsum("rjh,rjd->rhd", indicator_vector, gated, precision=lax.Precision.HIGHEST)
    weighted = weighted.astype(jnp.bfloat16).reshape(slot_rows, group_heads * head_width)
    head_contribution = jnp.dot(
        weighted,
        lax.all_gather(out_weight, "seq", axis=1, tiled=True),
        preferred_element_type=jnp.float32,
    ).astype(jnp.bfloat16)
    returned_rows = lax.all_to_all(
        head_contribution.reshape(groups, capacity, model_width),
        "grp",
        split_axis=0,
        concat_axis=0,
        tiled=True,
    )
    mixed = jnp.einsum("gct,gcd->td", by_slot_bf, returned_rows, preferred_element_type=jnp.float32)
    return mixed.astype(jnp.bfloat16)


def solution(mesh):
    in_specs = (
        P(("seq", "grp"), None),
        P(("seq", "grp"), None),
        P(("seq", "grp"), None),
        P(),
        P("seq", "grp"),
        P("grp", "seq"),
    )
    out_specs = P(("seq", "grp"), None)
    return jax.shard_map(
        on_device, mesh=mesh, in_specs=in_specs, out_specs=out_specs, check_vma=False
    )
```

profile of v0, /device:TPU:0, one launch (start us, length us, event | category | flops | bytes accessed | tf_op | source)
XLA Modules:
  0.0 367.7 jit_solution(14805347218649609205)
XLA Ops:
  6.5 0.7 all-gather.6.cloned.1.call-update
  7.3 0.0 all-gather.4.cloned.1.call-start
  7.3 0.4 copy-done
  7.8 4.6 %fusion.20 = bf16[128,4,256]{2,0,1:T(8,128)(2,1)S(1)} fusion(bf16[4096,4,256]{2,1,0:T(4,128)(2,1)} %param.13, bf16[128,4096]{1,0:T(8,128)(2,1)S(1)} %copy-done), kind=kOutput, calls=%fused_computation.27 | convolution fusion | flops 1073872896 | bytes 9699328 | tf_op jit(solution)/shard_map/td,dgc->tgc/dot_general | solution.py:82
  12.4 10.2 %all_to_all.30 = bf16[128,4,256]{2,0,1:T(8,128)(2,1)} all-to-all(bf16[128,4,256]{2,0,1:T(8,128)(2,1)S(1)} %fusion.20), channel_id=1, replica_groups=mesh['seq'=8,'grp'=4] {'grp'}, dimensions={1} | all-to-all | bytes 524288 | tf_op jit(solution)/shard_map/all_to_all | solution.py:128
  22.6 0.0 all-gather.4.cloned.1.call-update
  22.6 0.0 all-gather.8.cloned.1.call-start
  22.7 0.7 all-gather.8.cloned.1.call-update
  23.4 0.1 copy.85
  23.5 0.2 reduce_window_sum.22
  23.7 0.1 copy.95
  23.9 0.1 select_reduce_fusion.2
  23.9 0.1 select_reduce_fusion
  24.1 0.5 multiply_reduce_fusion.1
  24.6 0.6 pad_add_fusion
  25.3 3.3 all-to-all-start
  28.5 2.7 convolution_convert_fusion.1
  31.2 1.1 all-to-all-done
  32.3 4.7 %all-to-all-start.2 = ((bf16[4,96,4096]{2,1,0:T(8,128)(2,1)}), bf16[4,96,4096]{2,1,0:T(8,128)(2,1)}, u32[]{:S(2)}, u32[]{:S(2)}) async-start(bf16[4,96,4096]{2,1,0:T(8,128)(2,1)} %convolution_convert_fusion.1), calls=%async_computation.2 | async-start | bytes 6291456 | tf_op jit(solution)/shard_map/all_to_all | solution.py:102
  37.1 0.1 reshape.80
  37.2 0.1 copy.89
  37.3 0.1 copy.93
  37.5 0.6 broadcast_reduce_fusion
  38.1 99.0 %all-gather.6.cloned.1.call-done = bf16[4096,1024]{1,0:T(8,128)(2,1)} async-done(((bf16[512,1024]{1,0:T(8,128)(2,1)}), bf16[4096,1024]{1,0:T(8,128)(2,1)}) %all-gather.6.cloned.1.call-update) | async-done | bytes 8388624 | tf_op jit(solution)/shard_map/all_gather | solution.py:113
  137.1 11.3 %copy.91 = bf16[1024,4096]{1,0:T(8,128)(2,1)} copy(bf16[1024,4096]{0,1:T(8,128)(2,1)} %bitcast.45) | data formatting | bytes 16777216 | tf_op jit(solution)/shard_map/dot_general | solution.py:111
  148.4 6.9 %fusion.41 = f32[384,8,128]{2,0,1:T(8,128)S(1)} fusion(bf16[384,4096,1]{1,0,2:T(8,128)(2,1)} %bitcast.12, bf16[8,128,4096]{2,1,0:T(8,128)(2,1)} %bitcast.46), kind=kOutput, calls=%fused_computation.69 | convolution fusion | flops 3221225472 | bytes 13107200 | tf_op jit(solution)/shard_map/dot_general | solution.py:111
  155.3 3.2 fusion.17
  158.5 0.2 reshape.83
  158.7 28.2 %all-gather.4.cloned.1.call-done = bf16[4096,256]{1,0:T(8,128)(2,1)} async-done(((bf16[512,256]{1,0:T(8,128)(2,1)}), bf16[4096,256]{1,0:T(8,128)(2,1)}) %all-gather.4.cloned.1.call-update) | async-done | bytes 2097168 | tf_op jit(solution)/shard_map/all_gather | solution.py:139
  187.0 17.5 %while.15 = (s32[]{:T(128)}, f32[1152]{0:T(1024)S(1)}, f32[1152]{0:T(1024)S(1)}, f32[1152,128]{1,0:T(8,128)S(1)}, s32[4]{0:T(128)S(1)}, /*index=5*/s32[]{:T(128)...) while((s32[]{:T(128)}, f32[1152]{0:T(1024)S(1)}, ...), condition=%wide.region_14.15_spmd.clone, body=%wide.region_9.14_spmd.clone.sunk | while | flops 618433792 | bytes 35148632 | solution.py:68
  187.0 0.6 dynamic_slice.14
  188.9 9.7 %conditional.3 = ((f32[1152]{0:T(1024)S(1)}, f32[1152]{0:T(1024)S(1)}, f32[1152,128]{1,0:T(8,128)S(1)})) conditional(s32[]{:T(128)} %convert_element_type.92, (f32[1152]{0:T(1024)S(1)}, f32[1152]{0:T(1024)S(1)}, f32[1152,128]{1,0:T(8,128)S(1)}) %tuple.44, (s32[]{:T(128)}, s32[384]{0:T(512)S(1)}, bf16[4096,256]{1,0:T(8,128)(2,1)}, ...), branch_computations={%region_10.10_spmd, %region_11.13_spmd} | conditional | flops 618433792 | bytes 35148408 | solution.py:60
  188.9 0.1 broadcast_in_dim.57
  189.0 0.2 le.23
  189.2 1.8 fusion.40
  191.1 2.1 copy-done.1
  193.2 1.0 fusion.3
  194.2 4.3 %convolution_add_fusion = f32[1152,128]{1,0:T(8,128)S(1)} fusion(f32[1152,1024]{0,1:T(8,128)} %copy-done.1, f32[1152]{0:T(1024)S(1)} %max.4, s32[1152]{0:T(1024)S(1)} %le.23, s32[1024]{0:T(1024)S(1)} %iota_add_fusion, f32[1152,128]{1,0:T(8,128)S(1)} %get-tuple-element.117, f32[1152]{0:T(1024)S(1)} %get-tuple-element.183, ...), kind=kOutput, calls=%fused_computation.6 | convolution fusion | flops 307003392 | bytes 6178312 | tf_op jit(solution)/shard_map/while/body/eval_jaxpr/cond/branch_1_fun/dot_general | solution.py:52
  198.6 0.6 dynamic_slice.14
  200.5 0.6 dynamic_slice.14
  202.4 0.6 dynamic_slice.14
  204.5 0.2 broadcast_divide_fusion
  204.7 0.3 reshape.84
  205.0 3.5 convolution_convert_fusion.2
  208.4 104.5 %all-gather.8.cloned.1.call-done = bf16[1024,4096]{1,0:T(8,128)(2,1)} async-done(((bf16[1024,512]{1,0:T(8,128)(2,1)}), bf16[1024,4096]{1,0:T(8,128)(2,1)}) %all-gather.8.cloned.1.call-update) | async-done | bytes 8388624 | tf_op jit(solution)/shard_map/all_gather | solution.py:147
  312.9 7.1 %convolution_convert_fusion = bf16[384,4096]{1,0:T(8,128)(2,1)S(1)} fusion(bf16[1024,4096]{1,0:T(8,128)(2,1)} %all-gather.8.cloned.1.call-done, bf16[48,8,8,128]{3,2,1,0:T(8,128)(2,1)} %bitcast.56), kind=kOutput, calls=%fused_computation.19 | convolution fusion | flops 3222798336 | bytes 12320768 | tf_op jit(solution)/shard_map/dot_general | solution.py:145
  320.0 39.5 %all_to_all.31 = bf16[4,96,4096]{2,1,0:T(8,128)(2,1)S(1)} all-to-all(bf16[4,96,4096]{2,1,0:T(8,128)(2,1)S(1)} %bitcast.47), channel_id=1, replica_groups=mesh['seq'=8,'grp'=4] {'grp'}, dimensions={0} | all-to-all | bytes 6291456 | tf_op jit(solution)/shard_map/all_to_all | solution.py:150
  359.4 1.7 fusion.14
  (33 shorter events, 0.3 us)
Async XLA Ops:
  6.5 1.2 copy-start
  6.5 130.6 %all-gather.6.cloned.1.call-start = ((), (), s32[]{:S(2)}) async-start(), calls=%async_computation.5 | async-start | bytes 9437184 | tf_op jit(solution)/shard_map/all_gather | solution.py:113
  7.3 16.1 %copy-start.2 = (s32[128,4]{0,1:T(4,128)S(1)}, s32[128,4]{0,1:T(4,128)}, u32[]{:S(2)}) copy-start(s32[128,4]{0,1:T(4,128)} %param.11) | copy-start | bytes 6148
  7.3 16.6 %copy-start.3 = (s32[128,4]{0,1:T(4,128)S(1)}, s32[128,4]{0,1:T(4,128)}, u32[]{:S(2)}) copy-start(s32[128,4]{0,1:T(4,128)} %param.12) | copy-start | bytes 6148
  7.3 179.6 %all-gather.4.cloned.1.call-start = ((), (), s32[]{:S(2)}) async-start(), calls=%async_computation.4 | async-start | bytes 2359296 | tf_op jit(solution)/shard_map/all_gather | solution.py:139
  22.6 290.3 %all-gather.8.cloned.1.call-start = ((), (), s32[]{:S(2)}) async-start(), calls=%async_computation.6 | async-start | bytes 9437184 | tf_op jit(solution)/shard_map/all_gather | solution.py:147
  25.3 7.1 %all-to-all-start = ((s32[4,96,7]{1,2,0:T(8,128)}), s32[4,96,7]{1,2,0:T(8,128)S(1)}, u32[]{:S(2)}, u32[]{:S(2)}) async-start(s32[4,96,7]{1,2,0:T(8,128)} %pad_add_fusion), calls=%async_computation | async-start | bytes 32768 | tf_op jit(solution)/shard_map/all_to_all | solution.py:103
  32.3 116.1 %all-to-all-start.2 = ((bf16[4,96,4096]{2,1,0:T(8,128)(2,1)}), bf16[4,96,4096]{2,1,0:T(8,128)(2,1)}, u32[]{:S(2)}, u32[]{:S(2)}) async-start(bf16[4,96,4096]{2,1,0:T(8,128)(2,1)} %convolution_convert_fusion.1), calls=%async_computation.2 | async-start | bytes 6291456 | tf_op jit(solution)/shard_map/all_to_all | solution.py:102
  191.1 2.2 copy-start.1
Sparse Core Ops, SparseCore 0:
  9.5 127.6 all-gather.5
  139.3 47.6 all-gather.3
  189.0 123.8 all-gather.7
where the time goes:
time: 368 us
  waiting for transfers between devices  234 us (64%)
  blocking collectives  49.7 us (14%)
  matrix products  35.8 us (10%)
  local copies, waits for them, and re-layouts  17.7 us (5%)
  between operations  13.3 us (4%)
  starting transfers between devices  8.04 us (2%)
  loops' own time  5.43 us (1%)
    all_gather x1, waiting for transfers between devices, on_device(): lax.all_gather(out_weight, 'seq', axis=1, tiled=True)  104 us
    all_gather x1, waiting for transfers between devices, on_device(): lax.all_gather(query_weight, 'seq', axis=0, tiled=True)  99 us
    all_to_all x1, blocking collectives, on_device(): lax.all_to_all(head_contribution.reshape(groups, capacity, model_width),...  39.5 us
    all_gather x1, waiting for transfers between devices, on_device(): lax.all_gather(kv_group, 'seq', axis=0, tiled=True)  28.2 us
    dot_general x1, local copies, waits for them, and re-layouts, on_device(): jnp.dot(place_entries, lax.all_gather(query_weight, 'seq', axis=0, tiled=...  11.3 us
    all_to_all x1, blocking collectives, on_device(): lax.all_to_all(kv_local, 'grp', split_axis=1, concat_axis=0, tiled=True)  10.2 us
  transfers between devices with their start and end apart: 5, of which 4 were waited for; matrix products, arithmetic and copies ran while one was open for 12% of the time, Pallas kernels for 0%

commit v1 on v0

v1 whole, which is shorter than its diff:
```python
import functools

import jax
import jax.numpy as jnp
from jax import lax
from jax.experimental import pallas as pl
from jax.experimental.pallas import tpu as pltpu
from jax.sharding import PartitionSpec as P


def route_tables(head_index, gate_fixed, groups, capacity, group_heads):
    slots = head_index.shape[1] - 1
    cluster_membership = head_index // group_heads
    local_head = head_index % group_heads
    in_group = cluster_membership[:, None, :] == jnp.arange(groups, dtype=jnp.int32)[None, :, None]
    slot_order = jnp.cumsum(in_group.astype(jnp.int32), axis=2) - 1
    picked = (
        in_group[:, :, :, None] & (slot_order[:, :, :, None] == jnp.arange(slots, dtype=jnp.int32))
    ).astype(jnp.int32)
    slot_head = jnp.sum(picked * local_head[:, None, :, None], axis=2)
    slot_gate = jnp.sum(picked * gate_fixed[:, None, :, None], axis=2)
    member = jnp.any(in_group, axis=2).astype(jnp.int32)
    ranking = jnp.cumsum(member, axis=0) - 1
    retained = (member > 0) & (ranking < capacity)
    selected = (
        retained[:, :, None] & (ranking[:, :, None] == jnp.arange(capacity, dtype=jnp.int32))
    ).astype(jnp.int32)
    return (selected, slot_head, slot_gate)


MESH = pl.DeviceIdType.MESH
KV, WQ, WO = 0, 1, 2


def kernel(
    nz, nx, ng, group_heads, slots,
    rows_in, kv_in, wq_in, wo_in, heads_ref, gates_ref, pos_ref, sel_ref,
    out_ref,
    rows, kvs, wq, wo, q_all, queries, acc, top, total, weighted, contrib, back,
    local_sem, row_send, row_recv, kv_send, kv_recv, gather_send, gather_recv, back_send, back_recv,
):
    nb = nz * nx
    s, g = lax.axis_index("seq"), lax.axis_index("grp")
    z, x = s // nx, s % nx
    _, cap, width = rows.shape
    slot_rows = ng * cap
    depth = wq.shape[1]
    out_cols = wo.shape[2]
    tok = kvs.shape[2]
    keys = ng * tok
    hd = kvs.shape[3] // 2
    bufs = (kvs, wq, wo)

    def xs(k):
        return (z * nx + (x + k) % nx, g)

    def peer(k):
        return (g + k) % ng

    barrier = pltpu.get_barrier_semaphore()

    def greet(dev):
        pl.semaphore_signal(barrier, inc=1, device_id=dev, device_id_type=MESH)

    for k in range(1, nx):
        greet(xs(k))
    for k in range(1, ng):
        greet((s, peer(k)))

    @pl.when(z > 0)
    def _():
        greet((s - nx, g))

    @pl.when(z < nz - 1)
    def _():
        greet((s + nx, g))

    peers = nx - 1 + ng - 1 + (z > 0).astype(jnp.int32) + (z < nz - 1).astype(jnp.int32)
    pl.semaphore_wait(barrier, peers)

    own = [
        pltpu.make_async_copy(wq_in, wq.at[s], local_sem.at[0]),
        pltpu.make_async_copy(kv_in.at[g], kvs.at[s, g], local_sem.at[1]),
        pltpu.make_async_copy(rows_in.at[g], rows.at[g], local_sem.at[2]),
        pltpu.make_async_copy(wo_in, wo.at[s], local_sem.at[3]),
    ]
    for copy in own:
        copy.start()

    def kv_copy(k):
        to = peer(k)
        return pltpu.make_async_remote_copy(
            kv_in.at[to], kvs.at[s, g], kv_send.at[k - 1], kv_recv.at[k - 1], (s, to), MESH
        )

    def kv_arrival(k):
        frm = peer(ng - k)
        return pltpu.make_async_remote_copy(
            kv_in.at[g], kvs.at[s, frm], kv_send.at[k - 1], kv_recv.at[k - 1], (s, frm), MESH
        )

    def row_copy(k):
        to = peer(k)
        return pltpu.make_async_remote_copy(
            rows_in.at[to], rows.at[g], row_send.at[k - 1], row_recv.at[k - 1], (s, to), MESH
        )

    def row_arrival(k):
        frm = peer(ng - k)
        return pltpu.make_async_remote_copy(
            rows_in.at[g], rows.at[frm], row_send.at[k - 1], row_recv.at[k - 1], (s, frm), MESH
        )

    def gather(t, zz, kind, dev):
        b = zz * nx + x
        return pltpu.make_async_remote_copy(
            bufs[t].at[b], bufs[t].at[b],
            gather_send.at[(t * nz + zz) * (nx + 1) + kind],
            gather_recv.at[t * nb + b], dev, MESH,
        )

    def arrival(t, b):
        return pltpu.make_async_remote_copy(
            bufs[t].at[b], bufs[t].at[b], gather_send.at[0], gather_recv.at[t * nb + b],
            (s, peer(1)), MESH,
        )

    def across(t, zz):
        for k in range(1, nx):
            gather(t, zz, 1 + k, xs(k)).start()

    def up(t, zz):
        @pl.when(z < nz - 1)
        def _():
            gather(t, zz, 0, (s + nx, g)).start()

    def down(t, zz):
        @pl.when(z > 0)
        def _():
            gather(t, zz, 1, (s - nx, g)).start()

    def send_own(t):
        up(t, z)
        down(t, z)
        across(t, z)

    def stage(t, d):
        @pl.when(z - d >= 0)
        def _():
            arrival(t, (z - d) * nx + x).wait_recv()
            up(t, z - d)
            across(t, z - d)

        @pl.when(z + d < nz)
        def _():
            arrival(t, (z + d) * nx + x).wait_recv()
            down(t, z + d)
            across(t, z + d)

    for k in range(1, ng):
        kv_copy(k).start()
    own[0].wait()
    send_own(WQ)
    for k in range(1, ng):
        row_copy(k).start()
    own[1].wait()
    for k in range(1, ng):
        kv_arrival(k).wait_recv()
    send_own(KV)
    own[2].wait()
    own[3].wait()
    for d in range(1, nz):
        stage(KV, d)
        stage(WQ, d)
    send_own(WO)

    for k in range(1, ng):
        row_arrival(k).wait_recv()

    def block_at(i):
        flip = jnp.where(z * 2 < nz, i % nz, nz - 1 - i % nz)
        return flip * nx + (x + i // nz) % nx

    q_all[...] = jnp.zeros_like(q_all)

    def project(i, carry):
        b = block_at(i)

        @pl.when(i >= nz)
        def _():
            arrival(WQ, b).wait_recv()

        piece = rows[:, :, pl.ds(pl.multiple_of(b * depth, 128), depth)].reshape(slot_rows, depth)
        q_all[...] += jnp.dot(piece, wq[b], preferred_element_type=jnp.float32)
        return carry

    lax.fori_loop(0, nb, project, 0)

    for j in range(slots):
        head = heads_ref[:, j : j + 1]
        q = jnp.zeros((slot_rows, hd), jnp.float32)
        for h in range(group_heads):
            q = jnp.where(head == h, q_all[:, h * hd : (h + 1) * hd], q)
        queries[j] = q.astype(jnp.bfloat16)

    for i in range(nz, nb):
        arrival(KV, block_at(i)).wait_recv()

    def update(j, b, masked):
        k = kvs[b, :, :, :hd].reshape(keys, hd)
        v = kvs[b, :, :, hd:].reshape(keys, hd)
        scores = lax.dot_general(
            queries[j], k, (((1,), (1,)), ((), ())), preferred_element_type=jnp.float32
        ) * (hd ** -0.5)
        if masked:
            key_pos = b * keys + lax.broadcasted_iota(jnp.int32, scores.shape, 1)
            scores = jnp.where(key_pos <= pos_ref[...], scores, -1e30)
        before = top[...]
        newest = jnp.maximum(before, jnp.max(scores, axis=1, keepdims=True))
        weights = jnp.exp(scores - newest)
        factor = jnp.exp(before - newest)
        total[...] = total[...] * factor + jnp.sum(weights, axis=1, keepdims=True)
        acc[j] = acc[j] * factor + jnp.dot(
            weights.astype(jnp.bfloat16), v, preferred_element_type=jnp.float32
        )
        top[...] = newest

    def attend(j):
        top[...] = jnp.full_like(top, -1e30)
        total[...] = jnp.zeros_like(total)
        acc[j] = jnp.zeros((slot_rows, hd), jnp.float32)

        def step(b, carry):
            update(j, b, False)
            return carry

        lax.fori_loop(0, s, step, 0)
        update(j, s, True)
        acc[j] = acc[j] / total[...] * gates_ref[:, j : j + 1]

    for n in range(max(nz - 1, slots)):
        if n < slots:
            attend(n)
        if n < nz - 1:
            stage(WO, n + 1)

    for h in range(group_heads):
        value = jnp.zeros((slot_rows, hd), jnp.float32)
        for j in range(slots):
            value += jnp.where(heads_ref[:, j : j + 1] == h, acc[j], 0.0)
        weighted[:, h * hd : (h + 1) * hd] = value.astype(jnp.bfloat16)

    def back_copy(b, k):
        to = peer(k)
        return pltpu.make_async_remote_copy(
            contrib.at[b, to], back.at[b, g],
            back_send.at[b * (ng - 1) + k - 1], back_recv.at[b * (ng - 1) + k - 1], (s, to), MESH,
        )

    def back_arrival(b, k):
        frm = peer(ng - k)
        return pltpu.make_async_remote_copy(
            contrib.at[b, g], back.at[b, frm],
            back_send.at[b * (ng - 1) + k - 1], back_recv.at[b * (ng - 1) + k - 1], (s, frm), MESH,
        )

    def give_back(i, carry):
        b = block_at(i)

        @pl.when(i >= nz)
        def _():
            arrival(WO, b).wait_recv()

        product = jnp.dot(weighted[...], wo[b], preferred_element_type=jnp.float32)
        contrib[b] = product.astype(jnp.bfloat16).reshape(ng, cap, out_cols)
        for k in range(1, ng):
            back_copy(b, k).start()
        back[b, g] = contrib[b, g]
        return carry

    lax.fori_loop(0, nb, give_back, 0)

    def combine(i, carry):
        b = block_at(i)
        for k in range(1, ng):
            back_arrival(b, k).wait_recv()
        mixed = jnp.dot(
            sel_ref[...], back[b].reshape(slot_rows, out_cols), preferred_element_type=jnp.float32
        )
        out_ref[:, pl.ds(pl.multiple_of(b * out_cols, 128), out_cols)] = mixed.astype(jnp.bfloat16)
        for k in range(1, ng):
            back_copy(b, k).wait_send()
        return carry

    lax.fori_loop(0, nb, combine, 0)

    for k in range(1, ng):
        kv_copy(k).wait_send()
        row_copy(k).wait_send()
    for t in (KV, WQ, WO):
        for zz in range(nz):
            @pl.when((zz <= z) & (z < nz - 1))
            def _():
                gather(t, zz, 0, (s + nx, g)).wait_send()

            @pl.when((zz >= z) & (z > 0))
            def _():
                gather(t, zz, 1, (s - nx, g)).wait_send()

            for k in range(1, nx):
                gather(t, zz, 1 + k, xs(k)).wait_send()


def on_device(nz, tokens, head_index, gate_fixed, kv_weight, query_weight, out_weight):
    groups = lax.axis_size("grp")
    nb = lax.axis_size("seq")
    nx = nb // nz
    tok_rows, model_width = tokens.shape
    capacity = 3 * tok_rows // groups
    head_width = kv_weight.shape[2] // 2
    group_heads = query_weight.shape[1] // head_width
    slots = head_index.shape[1] - 1
    offset = (lax.axis_index("seq") * groups + lax.axis_index("grp")) * tok_rows
    positions = offset + jnp.arange(tok_rows, dtype=jnp.int32)
    kv_local = jnp.einsum(
        "td,dgc->gtc", tokens, kv_weight, preferred_element_type=jnp.float32
    ).astype(jnp.bfloat16)
    selected, slot_head, slot_gate = route_tables(
        head_index, gate_fixed, groups, capacity, group_heads
    )
    by_slot = jnp.transpose(selected, (1, 2, 0))
    by_slot_bf = by_slot.astype(jnp.bfloat16)
    send_tokens = jnp.einsum(
        "gct,td->gcd", by_slot_bf, tokens, preferred_element_type=jnp.float32
    ).astype(jnp.bfloat16)
    send_pos = jnp.sum(by_slot * positions[None, None, :], axis=2)
    send_head = jnp.sum(
        by_slot[:, :, :, None] * jnp.transpose(slot_head, (1, 0, 2))[:, None, :, :], axis=2
    )
    send_gate = jnp.sum(
        by_slot[:, :, :, None] * jnp.transpose(slot_gate, (1, 0, 2))[:, None, :, :], axis=2
    )
    send_meta = jnp.concatenate([send_head, send_gate, send_pos[:, :, None]], axis=2)
    recv_meta = lax.all_to_all(send_meta, "grp", split_axis=0, concat_axis=0, tiled=True)
    slot_rows = groups * capacity
    recv_meta = recv_meta.reshape(slot_rows, 2 * slots + 1)
    heads = recv_meta[:, :slots]
    gates = recv_meta[:, slots : 2 * slots].astype(jnp.float32) / 32768.0
    slot_pos = recv_meta[:, 2 * slots :]
    sel = by_slot_bf.reshape(slot_rows, tok_rows).T
    bf, f32 = jnp.bfloat16, jnp.float32
    depth, q_cols = query_weight.shape
    out_cols = out_weight.shape[1]
    any_spec = pl.BlockSpec(memory_space=pl.ANY)
    vmem_spec = pl.BlockSpec(memory_space=pltpu.VMEM)
    dma = pltpu.SemaphoreType.DMA
    return pl.pallas_call(
        functools.partial(kernel, nz, nx, groups, group_heads, slots),
        out_shape=jax.ShapeDtypeStruct((tok_rows, model_width), bf),
        in_specs=[any_spec] * 4 + [vmem_spec] * 4,
        out_specs=vmem_spec,
        scratch_shapes=[
            pltpu.VMEM((groups, capacity, model_width), bf),
            pltpu.VMEM((nb, groups, tok_rows, 2 * head_width), bf),
            pltpu.VMEM((nb, depth, q_cols), bf),
            pltpu.VMEM((nb, q_cols, out_cols), bf),
            pltpu.VMEM((slot_rows, q_cols), f32),
            pltpu.VMEM((slots, slot_rows, head_width), bf),
            pltpu.VMEM((slots, slot_rows, head_width), f32),
            pltpu.VMEM((slot_rows, 1), f32),
            pltpu.VMEM((slot_rows, 1), f32),
            pltpu.VMEM((slot_rows, q_cols), bf),
            pltpu.VMEM((nb, groups, capacity, out_cols), bf),
            pltpu.VMEM((nb, groups, capacity, out_cols), bf),
            dma((4,)),
            dma((groups - 1,)),
            dma((groups - 1,)),
            dma((groups - 1,)),
            dma((groups - 1,)),
            dma((3 * nz * (nx + 1),)),
            dma((3 * nb,)),
            dma((nb * (groups - 1),)),
            dma((nb * (groups - 1),)),
        ],
        compiler_params=pltpu.CompilerParams(
            collective_id=0, has_side_effects=True, vmem_limit_bytes=56 * 2**20
        ),
    )(send_tokens, kv_local, query_weight, out_weight, heads, gates, slot_pos, sel)


def solution(mesh):
    in_specs = (
        P(("seq", "grp"), None),
        P(("seq", "grp"), None),
        P(("seq", "grp"), None),
        P(),
        P("seq", "grp"),
        P("grp", "seq"),
    )
    out_specs = P(("seq", "grp"), None)
    nz = 4 if mesh.shape["seq"] % 4 == 0 else 1
    return jax.shard_map(
        functools.partial(on_device, nz),
        mesh=mesh, in_specs=in_specs, out_specs=out_specs, check_vma=False,
    )
```

time: 368 us -> 240 us (0.65)
  waiting for transfers between devices: 234 us -> 0.01 us
  Pallas kernels: 0 us -> 218 us
  blocking collectives: 49.7 us -> 0 us
  matrix products: 35.8 us -> 7.99 us
  local copies, waits for them, and re-layouts: 17.7 us -> 3.81 us
  between operations: 13.3 us -> 0.08 us
  loops' own time: 5.43 us -> 0 us
  starting transfers between devices: 8.04 us -> 4.24 us
    all_gather x3 -> x0, waiting for transfers between devices: 232 us -> none  [the longest x1 104 us: on_device(): lax.all_gather(out_weight, 'seq', axis=1, tiled=True)]
    pallas_call x0 -> x1, Pallas kernels: none -> 218 us  [on_device(): pl.pallas_call(functools.partial(kernel, nz, nx, groups, group_heads, slo...]
    all_to_all x2 -> x0, blocking collectives: 49.7 us -> none  [the longest x1 39.5 us: on_device(): lax.all_to_all(head_contribution.reshape(groups, capacity, model_width),...]
    dot_general x8 -> x1, matrix products: 33.1 us -> 5.35 us  [on_device(): jnp.einsum('td,dgc->gtc', tokens, kv_weight, preferred_element_type=jnp.f...]
    dot_general x1 -> x0, local copies, waits for them, and re-layouts: 11.3 us -> none  [on_device(): jnp.dot(place_entries, lax.all_gather(query_weight, 'seq', axis=0, tiled=...]
    another operation x5 -> x0, loops' own time: 5.43 us -> none  [the longest x1 5.32 us: attend(): lax.scan(step, state, jnp.arange(key_count // key_block, dtype=jnp.int32))]
    all_to_all x1 -> x0, starting transfers between devices: 4.7 us -> none  [on_device(): lax.all_to_all(send_tokens, 'grp', split_axis=0, concat_axis=0, tiled=True)]
  transfers between devices with their start and end apart: 5 -> 1, of which waited for: 4 -> 0; matrix products, arithmetic and copies ran while one was open for 12% -> 4% of each run, Pallas kernels for 0% -> 0%
where the time goes in v1:
time: 240 us; the launch traced here: 239 us
  Pallas kernels  218 us (91%)
  matrix products  7.99 us (3%)
  other arithmetic  4.56 us (2%)
  starting transfers between devices  4.24 us (2%)
  local copies, waits for them, and re-layouts  3.81 us (2%)
    pallas_call x1, Pallas kernels, on_device(): pl.pallas_call(functools.partial(kernel, nz, nx, groups, group_heads, slo...  218 us
    dot_general x1, matrix products, on_device(): jnp.einsum('td,dgc->gtc', tokens, kv_weight, preferred_element_type=jnp.f...  5.35 us
  transfers between devices with their start and end apart: 1, of which 0 were waited for; matrix products, arithmetic and copies ran while one was open for 4% of the time, Pallas kernels for 0%

profile of v1, /device:TPU:0, one launch (start us, length us, event | category | flops | bytes accessed | tf_op | source)
XLA Modules:
  0.0 238.9 jit_solution(15850038372367658015)
XLA Ops:
  0.0 0.0 copy-start
  0.0 0.8 add_select_fusion
  0.9 0.1 copy.94
  1.0 0.2 reduce_window_sum.22
  1.2 0.1 copy.103
  1.3 0.1 select_reduce_fusion
  1.4 0.7 select_reduce_fusion.2
  2.2 0.5 multiply_reduce_fusion.1
  2.7 0.6 pad_add_fusion
  3.3 4.2 %all-to-all-start = ((s32[4,96,7]{1,2,0:T(8,128)}), s32[4,96,7]{1,2,0:T(8,128)S(1)}, u32[]{:S(2)}, u32[]{:S(2)}) async-start(s32[4,96,7]{1,2,0:T(8,128)} %pad_add_fusion), calls=%async_computation | async-start | bytes 32768 | tf_op jit(solution)/shard_map/all_to_all | solution.py:344
  7.5 0.1 eq.76
  7.6 0.2 copy.101
  7.8 0.1 copy.100
  8.0 0.0 copy-done
  8.0 2.6 %convolution_convert_fusion.rows_in = bf16[4,96,4096]{2,1,0:T(8,128)(2,1)} fusion(bf16[128,4096]{1,0:T(8,128)(2,1)S(1)} %copy-done, s32[4,128]{1,0:T(4,128)S(1)} %bitcast.30, pred[4,128]{1,0:T(4,128)(4,1)S(1)} %bitcast_and_fusion), kind=kOutput, calls=%fused_computation.2 | convolution fusion | flops 404422656 | bytes 4196864 | tf_op jit(solution)/shard_map/gct,td->gcd/dot_general | solution.py:333
  10.6 5.3 %fusion.5.kv_in = bf16[4,128,256]{2,1,0:T(8,128)(2,1)} fusion(bf16[4096,4,256]{2,1,0:T(4,128)(2,1)} %param.9, bf16[128,4096]{1,0:T(8,128)(2,1)S(1)} %copy-done), kind=kOutput, calls=%fused_computation.4 | convolution fusion | flops 1073872896 | bytes 9699328 | tf_op jit(solution)/shard_map/td,dgc->gtc/dot_general | solution.py:325
  16.0 0.7 fusion.13.sel_ref
  16.6 0.0 all-to-all-done
  16.6 0.1 copy.99
  16.8 0.0 copy-start.1
  16.8 0.8 slice.14.pos_ref
  17.6 0.8 fusion.10.gates_ref
  18.4 0.0 copy-done.1
  18.4 218.3 %shard_map.64 = bf16[128,4096]{1,0:T(8,128)(2,1)} custom-call(bf16[4,96,4096]{2,1,0:T(8,128)(2,1)} %convolution_convert_fusion.rows_in, bf16[4,128,256]{2,1,0:T(8,128)(2,1)} %fusion.5.kv_in, bf16[512,1024]{1,0:T(8,128)(2,1)} %wq_in.1, bf16[1024,512]{1,0:T(8,128)(2,1)} %wo_in.1, s32[384,3]{1,0:T(8,128)} %bitcast.24, f32[384,3]{1,0:T(8,128)} %fusion.10.gates_ref, ...), custom_call_target="tpu_custom_call" | custom-call | tf_op jit(solution)/shard_map/pallas_call | solution.py:357
  236.7 2.3 copy.111
  (12 shorter events, 0.2 us)
Async XLA Ops:
  0.0 8.0 %copy-start = (bf16[128,4096]{1,0:T(8,128)(2,1)S(1)}, bf16[128,4096]{1,0:T(8,128)(2,1)}, u32[]{:S(2)}) copy-start(bf16[128,4096]{1,0:T(8,128)(2,1)} %param.6) | copy-start | bytes 3145732
  3.3 13.3 %all-to-all-start = ((s32[4,96,7]{1,2,0:T(8,128)}), s32[4,96,7]{1,2,0:T(8,128)S(1)}, u32[]{:S(2)}, u32[]{:S(2)}) async-start(s32[4,96,7]{1,2,0:T(8,128)} %pad_add_fusion), calls=%async_computation | async-start | bytes 32768 | tf_op jit(solution)/shard_map/all_to_all | solution.py:344
  16.8 1.6 copy-start.1

commit v2 on v1

--- a/solution.py
+++ b/solution.py
@@ -38,6 +38,7 @@
     out_ref,
     rows, kvs, wq, wo, q_all, queries, acc, top, total, weighted, contrib, back,
     local_sem, row_send, row_recv, kv_send, kv_recv, gather_send, gather_recv, back_send, back_recv,
+    half_send, half_recv,
 ):
     nb = nz * nx
     s, g = lax.axis_index("seq"), lax.axis_index("grp")
@@ -111,23 +112,45 @@
             rows_in.at[g], rows.at[frm], row_send.at[k - 1], row_recv.at[k - 1], (s, frm), MESH
         )
 
-    def gather(t, zz, kind, dev):
-        b = zz * nx + x
-        return pltpu.make_async_remote_copy(
-            bufs[t].at[b], bufs[t].at[b],
+    def part(t, b, which):
+        if which is None:
+            return bufs[t].at[b]
+        rows_half = bufs[t].shape[1] // 2
+        return bufs[t].at[b, which * rows_half : (which + 1) * rows_half]
+
+    def is_end(zz):
+        return (zz == 0) | (zz == nz - 1)
+
+    def gather(t, zz, kind, dev, which=None):
+        here = part(t, zz * nx + x, which)
+        return pltpu.make_async_remote_copy(
+            here, here,
             gather_send.at[(t * nz + zz) * (nx + 1) + kind],
-            gather_recv.at[t * nb + b], dev, MESH,
-        )
-
-    def arrival(t, b):
-        return pltpu.make_async_remote_copy(
-            bufs[t].at[b], bufs[t].at[b], gather_send.at[0], gather_recv.at[t * nb + b],
-            (s, peer(1)), MESH,
-        )
-
-    def across(t, zz):
-        for k in range(1, nx):
-            gather(t, zz, 1 + k, xs(k)).start()
+            gather_recv.at[t * nb + zz * nx + x], dev, MESH,
+        )
+
+    def arrival(t, b, which=None):
+        here = part(t, b, which)
+        return pltpu.make_async_remote_copy(
+            here, here, gather_send.at[0], gather_recv.at[t * nb + b], (s, peer(1)), MESH
+        )
+
+    def half(t, way, k):
+        end = 0 if way == 0 else nz - 1
+        here = part(t, end * nx + (x + k) % nx, 1)
+        at = (t * 2 + way) * nx + k
+        to = s + nx if way == 0 else s - nx
+        return pltpu.make_async_remote_copy(
+            here, here, half_send.at[at], half_recv.at[at], (to, g), MESH
+        )
+
+    def half_arrival(t, way, k):
+        end = 0 if way == 0 else nz - 1
+        here = part(t, end * nx + (x + k) % nx, 1)
+        at = (t * 2 + way) * nx + k
+        return pltpu.make_async_remote_copy(
+            here, here, half_send.at[at], half_recv.at[at], (s, peer(1)), MESH
+        )
 
     def up(t, zz):
         @pl.when(z < nz - 1)
@@ -142,9 +165,21 @@
     def send_own(t):
         up(t, z)
         down(t, z)
-        across(t, z)
-
-    def stage(t, d):
+        for k in range(1, nx):
+            gather(t, z, 1 + k, xs(k)).start()
+
+    def across(t, zz):
+        @pl.when(is_end(zz))
+        def _():
+            for k in range(1, nx):
+                gather(t, zz, 1 + k, xs(k), 0).start()
+
+        @pl.when(jnp.logical_not(is_end(zz)))
+        def _():
+            for k in range(1, nx):
+                gather(t, zz, 1 + k, xs(k)).start()
+
+    def column_stage(t, d):
         @pl.when(z - d >= 0)
         def _():
             arrival(t, (z - d) * nx + x).wait_recv()
@@ -156,6 +191,47 @@
             arrival(t, (z + d) * nx + x).wait_recv()
             down(t, z + d)
             across(t, z + d)
+
+    def half_stage(t, e):
+        for way in (0, 1):
+            @pl.when(z == (e if way == 0 else nz - 1 - e))
+            def _():
+                for k in range(1, nx):
+                    if e == 0:
+                        arrival(t, z * nx + (x + k) % nx).wait_recv()
+                    else:
+                        half_arrival(t, way, k).wait_recv()
+                    half(t, way, k).start()
+
+    def stage(t, d):
+        column_stage(t, d)
+        if d == 1:
+            half_stage(t, 0)
+        if d < nz - 1:
+            half_stage(t, d)
+
+    def consume(t, zz, k):
+        b = zz * nx + (x + k) % nx
+
+        @pl.when((zz == z) & jnp.logical_not(is_end(z)))
+        def _():
+            arrival(t, b).wait_recv()
+
+        @pl.when((zz != z) & jnp.logical_not(is_end(zz)))
+        def _():
+            arrival(t, b).wait_recv()
+
+        @pl.when((zz != z) & is_end(zz))
+        def _():
+            arrival(t, b, 0).wait_recv()
+
+        @pl.when((zz == 0) & (z == nz - 1))
+        def _():
+            half_arrival(t, 0, k).wait_recv()
+
+        @pl.when((zz == nz - 1) & (z == 0))
+        def _():
+            half_arrival(t, 1, k).wait_recv()
 
     for k in range(1, ng):
         kv_copy(k).start()
@@ -177,18 +253,24 @@
     for k in range(1, ng):
         row_arrival(k).wait_recv()
 
+    def shard_at(i):
+        return jnp.where(z * 2 < nz, i % nz, nz - 1 - i % nz)
+
     def block_at(i):
-        flip = jnp.where(z * 2 < nz, i % nz, nz - 1 - i % nz)
-        return flip * nx + (x + i // nz) % nx
+        return shard_at(i) * nx + (x + i // nz) % nx
+
+    def consume_from(t, i):
+        for k in range(1, nx):
+            @pl.when(i // nz == k)
+            def _():
+                consume(t, shard_at(i), k)
 
     q_all[...] = jnp.zeros_like(q_all)
 
     def project(i, carry):
         b = block_at(i)
 
-        @pl.when(i >= nz)
-        def _():
-            arrival(WQ, b).wait_recv()
+        consume_from(WQ, i)
 
         piece = rows[:, :, pl.ds(pl.multiple_of(b * depth, 128), depth)].reshape(slot_rows, depth)
         q_all[...] += jnp.dot(piece, wq[b], preferred_element_type=jnp.float32)
@@ -203,8 +285,9 @@
             q = jnp.where(head == h, q_all[:, h * hd : (h + 1) * hd], q)
         queries[j] = q.astype(jnp.bfloat16)
 
-    for i in range(nz, nb):
-        arrival(KV, block_at(i)).wait_recv()
+    for k in range(1, nx):
+        for zz in range(nz):
+            consume(KV, zz, k)
 
     def update(j, b, masked):
         k = kvs[b, :, :, :hd].reshape(keys, hd)
@@ -267,9 +350,7 @@
     def give_back(i, carry):
         b = block_at(i)
 
-        @pl.when(i >= nz)
-        def _():
-            arrival(WO, b).wait_recv()
+        consume_from(WO, i)
 
         product = jnp.dot(weighted[...], wo[b], preferred_element_type=jnp.float32)
         contrib[b] = product.astype(jnp.bfloat16).reshape(ng, cap, out_cols)
@@ -307,8 +388,27 @@
             def _():
                 gather(t, zz, 1, (s - nx, g)).wait_send()
 
-            for k in range(1, nx):
-                gather(t, zz, 1 + k, xs(k)).wait_send()
+            if zz in (0, nz - 1):
+                for k in range(1, nx):
+                    @pl.when(z == zz)
+                    def _():
+                        gather(t, zz, 1 + k, xs(k)).wait_send()
+
+                    @pl.when(z != zz)
+                    def _():
+                        gather(t, zz, 1 + k, xs(k), 0).wait_send()
+            else:
+                for k in range(1, nx):
+                    gather(t, zz, 1 + k, xs(k)).wait_send()
+
+        for k in range(1, nx):
+            @pl.when(z < nz - 1)
+            def _():
+                half(t, 0, k).wait_send()
+
+            @pl.when(z > 0)
+            def _():
+                half(t, 1, k).wait_send()
 
 
 def on_device(nz, tokens, head_index, gate_fixed, kv_weight, query_weight, out_weight):
@@ -381,6 +481,8 @@
             dma((3 * nb,)),
             dma((nb * (groups - 1),)),
             dma((nb * (groups - 1),)),
+            dma((3 * 2 * nx,)),
+            dma((3 * 2 * nx,)),
         ],
         compiler_params=pltpu.CompilerParams(
             collective_id=0, has_side_effects=True, vmem_limit_bytes=56 * 2**20
@@ -398,7 +500,7 @@
         P("grp", "seq"),
     )
     out_specs = P(("seq", "grp"), None)
-    nz = 4 if mesh.shape["seq"] % 4 == 0 else 1
+    nz = 4 if mesh.shape["seq"] % 4 == 0 else mesh.shape["seq"]
     return jax.shard_map(
         functools.partial(on_device, nz),
         mesh=mesh, in_specs=in_specs, out_specs=out_specs, check_vma=False,

time: 240 us -> 234 us (0.975)
  Pallas kernels: 218 us -> 213 us
    pallas_call x1, Pallas kernels: 218 us -> 213 us  [on_device(): pl.pallas_call(functools.partial(kernel, nz, nx, groups, group_heads, slo...]
where the time goes in v2:
time: 234 us
  Pallas kernels  213 us (91%)
  matrix products  7.99 us (3%)
  other arithmetic  4.56 us (2%)
  starting transfers between devices  4.24 us (2%)
  local copies, waits for them, and re-layouts  3.81 us (2%)
    pallas_call x1, Pallas kernels, on_device(): pl.pallas_call(functools.partial(kernel, nz, nx, groups, group_heads, slo...  213 us
    dot_general x1, matrix products, on_device(): jnp.einsum('td,dgc->gtc', tokens, kv_weight, preferred_element_type=jnp.f...  5.35 us
  transfers between devices with their start and end apart: 1, of which 0 were waited for; matrix products, arithmetic and copies ran while one was open for 4% of the time, Pallas kernels for 0%

profile of v2, /device:TPU:0, one launch (start us, length us, event | category | flops | bytes accessed | tf_op | source)
XLA Modules:
  0.0 233.6 jit_solution(16818172178024819518)
XLA Ops:
  0.0 0.0 copy-start
  0.0 0.8 add_select_fusion
  0.9 0.1 copy.94
  1.0 0.2 reduce_window_sum.22
  1.2 0.1 copy.103
  1.3 0.1 select_reduce_fusion
  1.4 0.7 select_reduce_fusion.2
  2.2 0.5 multiply_reduce_fusion.1
  2.7 0.6 pad_add_fusion
  3.3 4.2 %all-to-all-start = ((s32[4,96,7]{1,2,0:T(8,128)}), s32[4,96,7]{1,2,0:T(8,128)S(1)}, u32[]{:S(2)}, u32[]{:S(2)}) async-start(s32[4,96,7]{1,2,0:T(8,128)} %pad_add_fusion), calls=%async_computation | async-start | bytes 32768 | tf_op jit(solution)/shard_map/all_to_all | solution.py:444
  7.5 0.1 eq.76
  7.6 0.2 copy.101
  7.8 0.1 copy.100
  8.0 0.0 copy-done
  8.0 2.6 %convolution_convert_fusion.rows_in = bf16[4,96,4096]{2,1,0:T(8,128)(2,1)} fusion(bf16[128,4096]{1,0:T(8,128)(2,1)S(1)} %copy-done, s32[4,128]{1,0:T(4,128)S(1)} %bitcast.30, pred[4,128]{1,0:T(4,128)(4,1)S(1)} %bitcast_and_fusion), kind=kOutput, calls=%fused_computation.2 | convolution fusion | flops 404422656 | bytes 4196864 | tf_op jit(solution)/shard_map/gct,td->gcd/dot_general | solution.py:433
  10.6 5.3 %fusion.5.kv_in = bf16[4,128,256]{2,1,0:T(8,128)(2,1)} fusion(bf16[4096,4,256]{2,1,0:T(4,128)(2,1)} %param.9, bf16[128,4096]{1,0:T(8,128)(2,1)S(1)} %copy-done), kind=kOutput, calls=%fused_computation.4 | convolution fusion | flops 1073872896 | bytes 9699328 | tf_op jit(solution)/shard_map/td,dgc->gtc/dot_general | solution.py:425
  16.0 0.7 fusion.13.sel_ref
  16.6 0.0 all-to-all-done
  16.6 0.1 copy.99
  16.8 0.0 copy-start.1
  16.8 0.8 slice.14.pos_ref
  17.6 0.8 fusion.10.gates_ref
  18.4 0.0 copy-done.1
  18.4 212.9 %shard_map.64 = bf16[128,4096]{1,0:T(8,128)(2,1)} custom-call(bf16[4,96,4096]{2,1,0:T(8,128)(2,1)} %convolution_convert_fusion.rows_in, bf16[4,128,256]{2,1,0:T(8,128)(2,1)} %fusion.5.kv_in, bf16[512,1024]{1,0:T(8,128)(2,1)} %wq_in.1, bf16[1024,512]{1,0:T(8,128)(2,1)} %wo_in.1, s32[384,3]{1,0:T(8,128)} %bitcast.24, f32[384,3]{1,0:T(8,128)} %fusion.10.gates_ref, ...), custom_call_target="tpu_custom_call" | custom-call | tf_op jit(solution)/shard_map/pallas_call | solution.py:457
  231.3 2.3 copy.111
  (12 shorter events, 0.2 us)
Async XLA Ops:
  0.0 8.0 %copy-start = (bf16[128,4096]{1,0:T(8,128)(2,1)S(1)}, bf16[128,4096]{1,0:T(8,128)(2,1)}, u32[]{:S(2)}) copy-start(bf16[128,4096]{1,0:T(8,128)(2,1)} %param.6) | copy-start | bytes 3145732
  3.3 13.3 %all-to-all-start = ((s32[4,96,7]{1,2,0:T(8,128)}), s32[4,96,7]{1,2,0:T(8,128)S(1)}, u32[]{:S(2)}, u32[]{:S(2)}) async-start(s32[4,96,7]{1,2,0:T(8,128)} %pad_add_fusion), calls=%async_computation | async-start | bytes 32768 | tf_op jit(solution)/shard_map/all_to_all | solution.py:444
  16.8 1.6 copy-start.1

commit v3 on v2

--- a/solution.py
+++ b/solution.py
@@ -34,11 +34,11 @@
 
 def kernel(
     nz, nx, ng, group_heads, slots,
-    rows_in, kv_in, wq_in, wo_in, heads_ref, gates_ref, pos_ref, sel_ref,
+    kv_in, wq_in, wo_in, tokens_ref, sel_ref, meta_in,
     out_ref,
     rows, kvs, wq, wo, q_all, queries, acc, top, total, weighted, contrib, back,
     local_sem, row_send, row_recv, kv_send, kv_recv, gather_send, gather_recv, back_send, back_recv,
-    half_send, half_recv,
+    half_send, half_recv, rows_in, meta, meta_send, meta_recv, sel_t,
 ):
     nb = nz * nx
     s, g = lax.axis_index("seq"), lax.axis_index("grp")
@@ -82,8 +82,7 @@
     own = [
         pltpu.make_async_copy(wq_in, wq.at[s], local_sem.at[0]),
         pltpu.make_async_copy(kv_in.at[g], kvs.at[s, g], local_sem.at[1]),
-        pltpu.make_async_copy(rows_in.at[g], rows.at[g], local_sem.at[2]),
-        pltpu.make_async_copy(wo_in, wo.at[s], local_sem.at[3]),
+        pltpu.make_async_copy(wo_in, wo.at[s], local_sem.at[2]),
     ]
     for copy in own:
         copy.start()
@@ -98,6 +97,18 @@
         frm = peer(ng - k)
         return pltpu.make_async_remote_copy(
             kv_in.at[g], kvs.at[s, frm], kv_send.at[k - 1], kv_recv.at[k - 1], (s, frm), MESH
+        )
+
+    def meta_copy(k):
+        to = peer(k)
+        return pltpu.make_async_remote_copy(
+            meta_in.at[to], meta.at[g], meta_send.at[k - 1], meta_recv.at[k - 1], (s, to), MESH
+        )
+
+    def meta_arrival(k):
+        frm = peer(ng - k)
+        return pltpu.make_async_remote_copy(
+            meta_in.at[g], meta.at[frm], meta_send.at[k - 1], meta_recv.at[k - 1], (s, frm), MESH
         )
 
     def row_copy(k):
@@ -238,20 +249,34 @@
     own[0].wait()
     send_own(WQ)
     for k in range(1, ng):
-        row_copy(k).start()
+        meta_copy(k).start()
     own[1].wait()
     for k in range(1, ng):
         kv_arrival(k).wait_recv()
     send_own(KV)
+
+    def pick(i, carry):
+        cols = pl.ds(pl.multiple_of(i * 512, 128), 512)
+        piece = jnp.dot(sel_ref[...], tokens_ref[:, cols], preferred_element_type=jnp.float32)
+        rows_in[:, :, cols] = piece.astype(jnp.bfloat16).reshape(ng, cap, 512)
+        return carry
+
+    lax.fori_loop(0, width // 512, pick, 0)
+    for k in range(1, ng):
+        row_copy(k).start()
+    rows[g] = rows_in[g]
+    meta[g] = meta_in[g]
+    sel_t[...] = sel_ref[...].astype(jnp.float32).T.astype(jnp.bfloat16)
     own[2].wait()
-    own[3].wait()
     for d in range(1, nz):
         stage(KV, d)
         stage(WQ, d)
-    send_own(WO)
+        if d == max(nz - 2, 1):
+            send_own(WO)
 
     for k in range(1, ng):
         row_arrival(k).wait_recv()
+        meta_arrival(k).wait_recv()
 
     def shard_at(i):
         return jnp.where(z * 2 < nz, i % nz, nz - 1 - i % nz)
@@ -276,10 +301,15 @@
         q_all[...] += jnp.dot(piece, wq[b], preferred_element_type=jnp.float32)
         return carry
 
-    lax.fori_loop(0, nb, project, 0)
+    lax.fori_loop(0, nz, project, 0)
+    column_stage(WO, 1)
+    lax.fori_loop(nz, nb, project, 0)
+
+    def meta_column(i):
+        return meta[:, :, i : i + 1].reshape(slot_rows, 1)
 
     for j in range(slots):
-        head = heads_ref[:, j : j + 1]
+        head = meta_column(j)
         q = jnp.zeros((slot_rows, hd), jnp.float32)
         for h in range(group_heads):
             q = jnp.where(head == h, q_all[:, h * hd : (h + 1) * hd], q)
@@ -297,7 +327,7 @@
         ) * (hd ** -0.5)
         if masked:
             key_pos = b * keys + lax.broadcasted_iota(jnp.int32, scores.shape, 1)
-            scores = jnp.where(key_pos <= pos_ref[...], scores, -1e30)
+            scores = jnp.where(key_pos <= meta_column(2 * slots), scores, -1e30)
         before = top[...]
         newest = jnp.maximum(before, jnp.max(scores, axis=1, keepdims=True))
         weights = jnp.exp(scores - newest)
@@ -319,18 +349,22 @@
 
         lax.fori_loop(0, s, step, 0)
         update(j, s, True)
-        acc[j] = acc[j] / total[...] * gates_ref[:, j : j + 1]
+        acc[j] = acc[j] / total[...] * (meta_column(slots + j).astype(jnp.float32) / 32768.0)
 
     for n in range(max(nz - 1, slots)):
         if n < slots:
             attend(n)
-        if n < nz - 1:
+        if n == 0:
+            half_stage(WO, 0)
+            if nz > 2:
+                half_stage(WO, 1)
+        elif n < nz - 1:
             stage(WO, n + 1)
 
     for h in range(group_heads):
         value = jnp.zeros((slot_rows, hd), jnp.float32)
         for j in range(slots):
-            value += jnp.where(heads_ref[:, j : j + 1] == h, acc[j], 0.0)
+            value += jnp.where(meta_column(j) == h, acc[j], 0.0)
         weighted[:, h * hd : (h + 1) * hd] = value.astype(jnp.bfloat16)
 
     def back_copy(b, k):
@@ -366,7 +400,7 @@
         for k in range(1, ng):
             back_arrival(b, k).wait_recv()
         mixed = jnp.dot(
-            sel_ref[...], back[b].reshape(slot_rows, out_cols), preferred_element_type=jnp.float32
+            sel_t[...], back[b].reshape(slot_rows, out_cols), preferred_element_type=jnp.float32
         )
         out_ref[:, pl.ds(pl.multiple_of(b * out_cols, 128), out_cols)] = mixed.astype(jnp.bfloat16)
         for k in range(1, ng):
@@ -378,6 +412,7 @@
     for k in range(1, ng):
         kv_copy(k).wait_send()
         row_copy(k).wait_send()
+        meta_copy(k).wait_send()
     for t in (KV, WQ, WO):
         for zz in range(nz):
             @pl.when((zz <= z) & (z < nz - 1))
@@ -429,10 +464,6 @@
         head_index, gate_fixed, groups, capacity, group_heads
     )
     by_slot = jnp.transpose(selected, (1, 2, 0))
-    by_slot_bf = by_slot.astype(jnp.bfloat16)
-    send_tokens = jnp.einsum(
-        "gct,td->gcd", by_slot_bf, tokens, preferred_element_type=jnp.float32
-    ).astype(jnp.bfloat16)
     send_pos = jnp.sum(by_slot * positions[None, None, :], axis=2)
     send_head = jnp.sum(
         by_slot[:, :, :, None] * jnp.transpose(slot_head, (1, 0, 2))[:, None, :, :], axis=2
@@ -441,13 +472,9 @@
         by_slot[:, :, :, None] * jnp.transpose(slot_gate, (1, 0, 2))[:, None, :, :], axis=2
     )
     send_meta = jnp.concatenate([send_head, send_gate, send_pos[:, :, None]], axis=2)
-    recv_meta = lax.all_to_all(send_meta, "grp", split_axis=0, concat_axis=0, tiled=True)
+    send_meta = jnp.pad(send_meta, ((0, 0), (0, 0), (0, 128 - send_meta.shape[2])))
     slot_rows = groups * capacity
-    recv_meta = recv_meta.reshape(slot_rows, 2 * slots + 1)
-    heads = recv_meta[:, :slots]
-    gates = recv_meta[:, slots : 2 * slots].astype(jnp.float32) / 32768.0
-    slot_pos = recv_meta[:, 2 * slots :]
-    sel = by_slot_bf.reshape(slot_rows, tok_rows).T
+    sel = by_slot.astype(jnp.bfloat16).reshape(slot_rows, tok_rows)
     bf, f32 = jnp.bfloat16, jnp.float32
     depth, q_cols = query_weight.shape
     out_cols = out_weight.shape[1]
@@ -457,7 +484,7 @@
     return pl.pallas_call(
         functools.partial(kernel, nz, nx, groups, group_heads, slots),
         out_shape=jax.ShapeDtypeStruct((tok_rows, model_width), bf),
-        in_specs=[any_spec] * 4 + [vmem_spec] * 4,
+        in_specs=[any_spec] * 3 + [vmem_spec] * 3,
         out_specs=vmem_spec,
         scratch_shapes=[
             pltpu.VMEM((groups, capacity, model_width), bf),
@@ -472,7 +499,7 @@
             pltpu.VMEM((slot_rows, q_cols), bf),
             pltpu.VMEM((nb, groups, capacity, out_cols), bf),
             pltpu.VMEM((nb, groups, capacity, out_cols), bf),
-            dma((4,)),
+            dma((3,)),
             dma((groups - 1,)),
             dma((groups - 1,)),
             dma((groups - 1,)),
@@ -483,11 +510,16 @@
             dma((nb * (groups - 1),)),
             dma((3 * 2 * nx,)),
             dma((3 * 2 * nx,)),
+            pltpu.VMEM((groups, capacity, model_width), bf),
+            pltpu.VMEM((groups, capacity, 128), jnp.int32),
+            dma((groups - 1,)),
+            dma((groups - 1,)),
+            pltpu.VMEM((tok_rows, slot_rows), bf),
         ],
         compiler_params=pltpu.CompilerParams(
             collective_id=0, has_side_effects=True, vmem_limit_bytes=56 * 2**20
         ),
-    )(send_tokens, kv_local, query_weight, out_weight, heads, gates, slot_pos, sel)
+    )(kv_local, query_weight, out_weight, tokens, sel, send_meta)
 
 
 def solution(mesh):

time: 234 us -> 226 us (0.966)
  starting transfers between devices: 4.24 us -> 0 us
    all_to_all x1 -> x0, starting transfers between devices: 4.24 us -> none  [on_device(): lax.all_to_all(send_meta, 'grp', split_axis=0, concat_axis=0, tiled=True)]
    dot_general x1 -> x0, matrix products: 2.64 us -> none  [on_device(): jnp.einsum('gct,td->gcd', by_slot_bf, tokens, preferred_element_type=jnp....]
  transfers between devices with their start and end apart: 1 -> 0, of which waited for: 0 -> 0; matrix products, arithmetic and copies ran while one was open for 4% -> 0% of each run, Pallas kernels for 0% -> 0%
where the time goes in v3:
time: 226 us
  Pallas kernels  213 us (94%)
  matrix products  5.69 us (3%)
  local copies, waits for them, and re-layouts  3.65 us (2%)
  other arithmetic  3.32 us (1%)
    pallas_call x1, Pallas kernels, on_device(): pl.pallas_call(functools.partial(kernel, nz, nx, groups, group_heads, slo...  213 us
    dot_general x1, matrix products, on_device(): jnp.einsum('td,dgc->gtc', tokens, kv_weight, preferred_element_type=jnp.f...  5.69 us

profile of v3, /device:TPU:0, one launch (start us, length us, event | category | flops | bytes accessed | tf_op | source)
XLA Modules:
  0.0 225.9 jit_solution(8994125746522246103)
XLA Ops:
  0.0 0.1 eq.71
  0.1 0.7 add_select_fusion
  0.9 0.7 select_reduce_fusion.2
  1.6 0.1 copy.85
  1.7 0.2 reduce_window_sum.22
  1.9 0.1 copy.91
  2.0 0.2 select_reduce_fusion
  2.1 0.8 convert_convert_fusion.sel_ref
  2.9 0.5 multiply_reduce_fusion.1
  3.4 0.1 copy.87
  3.6 0.1 copy.89
  3.7 0.1 copy.88
  3.9 0.2 pad_add_fusion
  4.0 0.7 pad.4.meta_in
  4.7 5.7 %fusion.5.kv_in = bf16[4,128,256]{2,1,0:T(8,128)(2,1)} fusion(bf16[4096,4,256]{2,1,0:T(4,128)(2,1)} %param.9, bf16[128,4096]{1,0:T(8,128)(2,1)} %tokens_ref.1), kind=kOutput, calls=%fused_computation.3 | convolution fusion | flops 1073872896 | bytes 9699328 | tf_op jit(solution)/shard_map/td,dgc->gtc/dot_general | solution.py:460
  10.4 213.2 %shard_map.64 = bf16[128,4096]{1,0:T(8,128)(2,1)} custom-call(bf16[4,128,256]{2,1,0:T(8,128)(2,1)} %fusion.5.kv_in, bf16[512,1024]{1,0:T(8,128)(2,1)} %wq_in.1, bf16[1024,512]{1,0:T(8,128)(2,1)} %wo_in.1, bf16[128,4096]{1,0:T(8,128)(2,1)} %tokens_ref.1, bf16[384,128]{1,0:T(8,128)(2,1)} %convert_convert_fusion.sel_ref, s32[4,96,128]{2,1,0:T(8,128)} %pad.4.meta_in), custom_call_target="tpu_custom_call" | custom-call | tf_op jit(solution)/shard_map/pallas_call | solution.py:484
  223.7 2.3 %copy.99 = bf16[128,4096]{1,0:T(8,128)(2,1)} copy(bf16[128,4096]{1,0:T(8,128)(2,1)} %shard_map.64) | data formatting | bytes 2097152
  (10 shorter events, 0.1 us)

commit v4 on v3

--- a/solution.py
+++ b/solution.py
@@ -271,8 +271,13 @@
     for d in range(1, nz):
         stage(KV, d)
         stage(WQ, d)
+        if d == 1:
+            send_own(WO)
         if d == max(nz - 2, 1):
-            send_own(WO)
+            column_stage(WO, 1)
+    half_stage(WO, 0)
+    if nz > 2:
+        half_stage(WO, 1)
 
     for k in range(1, ng):
         row_arrival(k).wait_recv()
@@ -301,9 +306,7 @@
         q_all[...] += jnp.dot(piece, wq[b], preferred_element_type=jnp.float32)
         return carry
 
-    lax.fori_loop(0, nz, project, 0)
-    column_stage(WO, 1)
-    lax.fori_loop(nz, nb, project, 0)
+    lax.fori_loop(0, nb, project, 0)
 
     def meta_column(i):
         return meta[:, :, i : i + 1].reshape(slot_rows, 1)
@@ -354,11 +357,7 @@
     for n in range(max(nz - 1, slots)):
         if n < slots:
             attend(n)
-        if n == 0:
-            half_stage(WO, 0)
-            if nz > 2:
-                half_stage(WO, 1)
-        elif n < nz - 1:
+        if 0 < n < nz - 1:
             stage(WO, n + 1)
 
     for h in range(group_heads):

time: 226 us -> 226 us (level)
  no operation moved by 1% of the time
where the time goes in v4:
time: 226 us
  Pallas kernels  213 us (94%)
  matrix products  5.69 us (3%)
  local copies, waits for them, and re-layouts  3.65 us (2%)
  other arithmetic  3.32 us (1%)
    pallas_call x1, Pallas kernels, on_device(): pl.pallas_call(functools.partial(kernel, nz, nx, groups, group_heads, slo...  213 us
    dot_general x1, matrix products, on_device(): jnp.einsum('td,dgc->gtc', tokens, kv_weight, preferred_element_type=jnp.f...  5.69 us

profile of v4, /device:TPU:0, one launch (start us, length us, event | category | flops | bytes accessed | tf_op | source)
XLA Modules:
  0.0 225.9 jit_solution(3071739971047113475)
XLA Ops:
  0.0 0.1 eq.71
  0.1 0.7 add_select_fusion
  0.9 0.7 select_reduce_fusion.2
  1.6 0.1 copy.85
  1.7 0.2 reduce_window_sum.22
  1.9 0.1 copy.91
  2.0 0.2 select_reduce_fusion
  2.1 0.8 convert_convert_fusion.sel_ref
  2.9 0.5 multiply_reduce_fusion.1
  3.4 0.1 copy.87
  3.6 0.1 copy.89
  3.7 0.1 copy.88
  3.9 0.2 pad_add_fusion
  4.0 0.7 pad.4.meta_in
  4.7 5.7 %fusion.5.kv_in = bf16[4,128,256]{2,1,0:T(8,128)(2,1)} fusion(bf16[4096,4,256]{2,1,0:T(4,128)(2,1)} %param.9, bf16[128,4096]{1,0:T(8,128)(2,1)} %tokens_ref.1), kind=kOutput, calls=%fused_computation.3 | convolution fusion | flops 1073872896 | bytes 9699328 | tf_op jit(solution)/shard_map/td,dgc->gtc/dot_general | solution.py:459
  10.4 213.2 %shard_map.64 = bf16[128,4096]{1,0:T(8,128)(2,1)} custom-call(bf16[4,128,256]{2,1,0:T(8,128)(2,1)} %fusion.5.kv_in, bf16[512,1024]{1,0:T(8,128)(2,1)} %wq_in.1, bf16[1024,512]{1,0:T(8,128)(2,1)} %wo_in.1, bf16[128,4096]{1,0:T(8,128)(2,1)} %tokens_ref.1, bf16[384,128]{1,0:T(8,128)(2,1)} %convert_convert_fusion.sel_ref, s32[4,96,128]{2,1,0:T(8,128)} %pad.4.meta_in), custom_call_target="tpu_custom_call" | custom-call | tf_op jit(solution)/shard_map/pallas_call | solution.py:483
  223.7 2.3 %copy.99 = bf16[128,4096]{1,0:T(8,128)(2,1)} copy(bf16[128,4096]{1,0:T(8,128)(2,1)} %shard_map.64) | data formatting | bytes 2097152
  (10 shorter events, 0.1 us)

commit v5 on v4

--- a/solution.py
+++ b/solution.py
@@ -354,11 +354,23 @@
         update(j, s, True)
         acc[j] = acc[j] / total[...] * (meta_column(slots + j).astype(jnp.float32) / 32768.0)
 
-    for n in range(max(nz - 1, slots)):
-        if n < slots:
-            attend(n)
-        if 0 < n < nz - 1:
-            stage(WO, n + 1)
+    def rest(last):
+        for d in range(2, last + 1):
+            stage(WO, d)
+
+    @pl.when(jnp.logical_not(is_end(z)))
+    def _():
+        rest(nz - 2)
+
+    for n in range(slots):
+        if n == slots - 1:
+            @pl.when(is_end(z))
+            def _():
+                rest(nz - 2)
+
+        attend(n)
+    if nz > 2:
+        stage(WO, nz - 1)
 
     for h in range(group_heads):
         value = jnp.zeros((slot_rows, hd), jnp.float32)

time: 226 us -> 226 us (level)
  no operation moved by 1% of the time
where the time goes in v5:
time: 226 us
  Pallas kernels  213 us (94%)
  matrix products  5.69 us (3%)
  local copies, waits for them, and re-layouts  3.65 us (2%)
  other arithmetic  3.32 us (1%)
    pallas_call x1, Pallas kernels, on_device(): pl.pallas_call(functools.partial(kernel, nz, nx, groups, group_heads, slo...  213 us
    dot_general x1, matrix products, on_device(): jnp.einsum('td,dgc->gtc', tokens, kv_weight, preferred_element_type=jnp.f...  5.69 us

profile of v5, /device:TPU:0, one launch (start us, length us, event | category | flops | bytes accessed | tf_op | source)
XLA Modules:
  0.0 225.9 jit_solution(18143076328782135337)
XLA Ops:
  0.0 0.1 eq.71
  0.1 0.7 add_select_fusion
  0.9 0.7 select_reduce_fusion.2
  1.6 0.1 copy.85
  1.7 0.2 reduce_window_sum.22
  1.9 0.1 copy.91
  2.0 0.2 select_reduce_fusion
  2.1 0.8 convert_convert_fusion.sel_ref
  2.9 0.5 multiply_reduce_fusion.1
  3.4 0.1 copy.87
  3.6 0.1 copy.89
  3.7 0.1 copy.88
  3.9 0.2 pad_add_fusion
  4.0 0.7 pad.4.meta_in
  4.7 5.7 %fusion.5.kv_in = bf16[4,128,256]{2,1,0:T(8,128)(2,1)} fusion(bf16[4096,4,256]{2,1,0:T(4,128)(2,1)} %param.9, bf16[128,4096]{1,0:T(8,128)(2,1)} %tokens_ref.1), kind=kOutput, calls=%fused_computation.3 | convolution fusion | flops 1073872896 | bytes 9699328 | tf_op jit(solution)/shard_map/td,dgc->gtc/dot_general | solution.py:471
  10.4 213.2 %shard_map.64 = bf16[128,4096]{1,0:T(8,128)(2,1)} custom-call(bf16[4,128,256]{2,1,0:T(8,128)(2,1)} %fusion.5.kv_in, bf16[512,1024]{1,0:T(8,128)(2,1)} %wq_in.1, bf16[1024,512]{1,0:T(8,128)(2,1)} %wo_in.1, bf16[128,4096]{1,0:T(8,128)(2,1)} %tokens_ref.1, bf16[384,128]{1,0:T(8,128)(2,1)} %convert_convert_fusion.sel_ref, s32[4,96,128]{2,1,0:T(8,128)} %pad.4.meta_in), custom_call_target="tpu_custom_call" | custom-call | tf_op jit(solution)/shard_map/pallas_call | solution.py:495
  223.7 2.3 %copy.99 = bf16[128,4096]{1,0:T(8,128)(2,1)} copy(bf16[128,4096]{1,0:T(8,128)(2,1)} %shard_map.64) | data formatting | bytes 2097152
  (10 shorter events, 0.1 us)
